TPU v7x, 256 devices: a whole 4x4x8 slice. The times are simulated.
256 devices in a mesh: blk: 32 (over z, y_lo, core), group: 8 (over x, y_hi).
Axes of the slice: x: 4, y: 4 (y_hi: 2, y_lo: 2; y = y_hi * 2 + y_lo), z: 8, core: 2. Of those that a mesh axis runs over, the one named last changes fastest.
Arguments:
- image_embed: bfloat16 [32768, 1152], P(('group', 'blk')), parts along dimension 0, may hold values from -0.5 to 0.5
- text_embed: bfloat16 [32768, 1152], P(('group', 'blk')), parts along dimension 0, may hold values from -0.5 to 0.5
- logit_scale: float32 [1], replicated, may hold values from 4 to 12
- logit_bias: float32 [1], replicated, may hold values from -4 to -1
Outputs:
- row_loss: float32 [32768], P(('group', 'blk')), parts along dimension 0
- image_grad: float32 [32768, 1152], P(('group', 'blk')), parts along dimension 0
- text_grad: float32 [32768, 1152], P(('group', 'blk')), parts along dimension 0
There are 8 independent parts, one for each index of `group`. A program takes and returns all parts, laid end to end along the dimension named above; an argument that names none is the same for every part. Nothing has to cross between parts.
All inputs are finite; a program needn't handle non-finite values.
Results may differ from a plain program's by a relative error of at most 0.0085.
Values may be sent and summed in bfloat16 or wider, within the bound.
A program may use at most 128 MiB of HBM per device.

v0:
```python
import jax
import jax.numpy as jnp
from jax import lax
from jax.sharding import PartitionSpec as P


def from_behind(block, axis, distance):
    devices = range(lax.axis_size(axis))
    route = [((i - distance) % len(devices), i) for i in devices]
    return lax.ppermute(block, axis, route)


def normalize(rows_in):
    values = rows_in.astype(jnp.float32)
    norm = jnp.sqrt(jnp.sum(values * values, axis=1, keepdims=True) + 1e-06)
    return (values / norm, norm)


def unnormal(grad, unit, norm):
    return (grad - unit * jnp.sum(unit * grad, axis=1, keepdims=True)) / norm


def score_tile(images, texts, sign, scale, bias):
    logits = (
        scale
        * lax.dot_general(
            images, texts, (((1,), (1,)), ((), ())), preferred_element_type=jnp.float32
        )
        + bias
    )
    loss = jnp.sum(jax.nn.softplus(-sign * logits), axis=1)
    coef = (-sign * jax.nn.sigmoid(-sign * logits)).astype(jnp.bfloat16)
    return (loss, coef)


def per_device(image_embed, text_embed, logit_scale, logit_bias):
    scale = logit_scale[0]
    bias = logit_bias[0]
    img_unit, img_norm = normalize(image_embed)
    txt_unit, txt_norm = normalize(text_embed)
    zi = img_unit.astype(jnp.bfloat16)
    zt = txt_unit.astype(jnp.bfloat16)
    rows = zi.shape[0]
    width = zi.shape[1]
    count = lax.axis_size("blk")
    row_ids = lax.broadcasted_iota(jnp.int32, (rows, rows), 0)
    col_ids = lax.broadcasted_iota(jnp.int32, (rows, rows), 1)
    diag_sign = jnp.where(row_ids == col_ids, jnp.float32(1.0), jnp.float32(-1.0))
    off_sign = jnp.full((rows, rows), -1.0, jnp.float32)
    empty = jnp.zeros((rows, width), jnp.float32)
    start_state = (jnp.zeros((rows,), jnp.float32), empty)

    def visit(state, block, grads, sign):
        loss_rows, g_img = state
        loss, coef = score_tile(zi, block, sign, scale, bias)
        g_img = g_img + scale * jnp.dot(coef, block, preferred_element_type=jnp.float32)
        grads = grads + scale * lax.dot_general(
            coef, zi, (((0,), (0,)), ((), ())), preferred_element_type=jnp.float32
        )
        return ((loss_rows + loss, g_img), grads)

    state, own = visit(start_state, zt, empty, diag_sign)

    def cycle_turn(step, carry):
        state, block, grads = carry
        block = from_behind(block, "blk", 1)
        grads = from_behind(grads, "blk", 1)
        state, grads = visit(state, block, grads, off_sign)
        return (state, block, grads)

    state, block, grads = lax.fori_loop(1, count, cycle_turn, (state, zt, own))
    g_txt = from_behind(grads, "blk", 1)
    row_loss, g_img = state
    return (row_loss, unnormal(g_img, img_unit, img_norm), unnormal(g_txt, txt_unit, txt_norm))


def solution(mesh):
    placed = (P(("group", "blk"), None), P(("group", "blk"), None), P(), P())
    return jax.shard_map(
        per_device,
        mesh=mesh,
        in_specs=placed,
        out_specs=(P(("group", "blk")), P(("group", "blk"), None), P(("group", "blk"), None)),
        check_vma=False,
    )
```

profile of v0, /device:TPU:2, one launch (start us, length us, event | category | flops | bytes accessed | tf_op | source)
XLA Modules:
  0.0 502.2 jit_solution(11711403286412579400)
XLA Ops:
  4.4 484.6 %while.16 = (s32[]{:T(128)}, f32[128]{0:T(128)S(1)}, f32[128,1152]{1,0:T(8,128)S(1)}, bf16[128,1152]{1,0:T(8,128)(2,1)S(1)}, f32[128,1152]{1,0:T(8,128)S(1)}, /*...) while((s32[]{:T(128)}, f32[128]{0:T(128)S(1)}, f32[128,1152]{1,0:T(8,128)S(1)}, ...), condition=%wide.region_5.6_spmd, body=%wide.region_3.5_spmd.sunk | while | flops 114114560 | bytes 7866557 | solution.py:71
  6.2 9.0 %collective-permute-done = bf16[128,1152]{1,0:T(8,128)(2,1)S(1)} collective-permute-done((bf16[128,1152]{1,0:T(8,128)(2,1)S(1)}, bf16[128,1152]{1,0:T(8,128)(2,1)S(1)}, u32[]{:S(2)}, u32[]{:S(2)}) %collective-permute-start) | collective-permute-done | bytes 294944 | tf_op jit(solution)/shard_map/while/body/eval_jaxpr/ppermute | solution.py:10
  17.8 3.7 collective-permute-done.1
  22.6 8.2 %collective-permute-done = bf16[128,1152]{1,0:T(8,128)(2,1)S(1)} collective-permute-done((bf16[128,1152]{1,0:T(8,128)(2,1)S(1)}, bf16[128,1152]{1,0:T(8,128)(2,1)S(1)}, u32[]{:S(2)}, u32[]{:S(2)}) %collective-permute-start) | collective-permute-done | bytes 294944 | tf_op jit(solution)/shard_map/while/body/eval_jaxpr/ppermute | solution.py:10
  33.3 3.7 collective-permute-done.1
  38.2 8.2 %collective-permute-done = bf16[128,1152]{1,0:T(8,128)(2,1)S(1)} collective-permute-done((bf16[128,1152]{1,0:T(8,128)(2,1)S(1)}, bf16[128,1152]{1,0:T(8,128)(2,1)S(1)}, u32[]{:S(2)}, u32[]{:S(2)}) %collective-permute-start) | collective-permute-done | bytes 294944 | tf_op jit(solution)/shard_map/while/body/eval_jaxpr/ppermute | solution.py:10
  48.9 3.7 collective-permute-done.1
  53.7 8.2 %collective-permute-done = bf16[128,1152]{1,0:T(8,128)(2,1)S(1)} collective-permute-done((bf16[128,1152]{1,0:T(8,128)(2,1)S(1)}, bf16[128,1152]{1,0:T(8,128)(2,1)S(1)}, u32[]{:S(2)}, u32[]{:S(2)}) %collective-permute-start) | collective-permute-done | bytes 294944 | tf_op jit(solution)/shard_map/while/body/eval_jaxpr/ppermute | solution.py:10
  64.4 3.7 collective-permute-done.1
  69.3 8.2 %collective-permute-done = bf16[128,1152]{1,0:T(8,128)(2,1)S(1)} collective-permute-done((bf16[128,1152]{1,0:T(8,128)(2,1)S(1)}, bf16[128,1152]{1,0:T(8,128)(2,1)S(1)}, u32[]{:S(2)}, u32[]{:S(2)}) %collective-permute-start) | collective-permute-done | bytes 294944 | tf_op jit(solution)/shard_map/while/body/eval_jaxpr/ppermute | solution.py:10
  80.0 3.7 collective-permute-done.1
  84.8 8.2 %collective-permute-done = bf16[128,1152]{1,0:T(8,128)(2,1)S(1)} collective-permute-done((bf16[128,1152]{1,0:T(8,128)(2,1)S(1)}, bf16[128,1152]{1,0:T(8,128)(2,1)S(1)}, u32[]{:S(2)}, u32[]{:S(2)}) %collective-permute-start) | collective-permute-done | bytes 294944 | tf_op jit(solution)/shard_map/while/body/eval_jaxpr/ppermute | solution.py:10
  95.5 3.7 collective-permute-done.1
  100.4 8.2 %collective-permute-done = bf16[128,1152]{1,0:T(8,128)(2,1)S(1)} collective-permute-done((bf16[128,1152]{1,0:T(8,128)(2,1)S(1)}, bf16[128,1152]{1,0:T(8,128)(2,1)S(1)}, u32[]{:S(2)}, u32[]{:S(2)}) %collective-permute-start) | collective-permute-done | bytes 294944 | tf_op jit(solution)/shard_map/while/body/eval_jaxpr/ppermute | solution.py:10
  111.1 3.7 collective-permute-done.1
  115.9 8.2 %collective-permute-done = bf16[128,1152]{1,0:T(8,128)(2,1)S(1)} collective-permute-done((bf16[128,1152]{1,0:T(8,128)(2,1)S(1)}, bf16[128,1152]{1,0:T(8,128)(2,1)S(1)}, u32[]{:S(2)}, u32[]{:S(2)}) %collective-permute-start) | collective-permute-done | bytes 294944 | tf_op jit(solution)/shard_map/while/body/eval_jaxpr/ppermute | solution.py:10
  126.7 3.7 collective-permute-done.1
  131.5 8.2 %collective-permute-done = bf16[128,1152]{1,0:T(8,128)(2,1)S(1)} collective-permute-done((bf16[128,1152]{1,0:T(8,128)(2,1)S(1)}, bf16[128,1152]{1,0:T(8,128)(2,1)S(1)}, u32[]{:S(2)}, u32[]{:S(2)}) %collective-permute-start) | collective-permute-done | bytes 294944 | tf_op jit(solution)/shard_map/while/body/eval_jaxpr/ppermute | solution.py:10
  142.2 3.7 collective-permute-done.1
  147.0 8.2 %collective-permute-done = bf16[128,1152]{1,0:T(8,128)(2,1)S(1)} collective-permute-done((bf16[128,1152]{1,0:T(8,128)(2,1)S(1)}, bf16[128,1152]{1,0:T(8,128)(2,1)S(1)}, u32[]{:S(2)}, u32[]{:S(2)}) %collective-permute-start) | collective-permute-done | bytes 294944 | tf_op jit(solution)/shard_map/while/body/eval_jaxpr/ppermute | solution.py:10
  157.8 3.7 collective-permute-done.1
  162.6 8.2 %collective-permute-done = bf16[128,1152]{1,0:T(8,128)(2,1)S(1)} collective-permute-done((bf16[128,1152]{1,0:T(8,128)(2,1)S(1)}, bf16[128,1152]{1,0:T(8,128)(2,1)S(1)}, u32[]{:S(2)}, u32[]{:S(2)}) %collective-permute-start) | collective-permute-done | bytes 294944 | tf_op jit(solution)/shard_map/while/body/eval_jaxpr/ppermute | solution.py:10
  173.3 3.7 collective-permute-done.1
  178.1 8.2 %collective-permute-done = bf16[128,1152]{1,0:T(8,128)(2,1)S(1)} collective-permute-done((bf16[128,1152]{1,0:T(8,128)(2,1)S(1)}, bf16[128,1152]{1,0:T(8,128)(2,1)S(1)}, u32[]{:S(2)}, u32[]{:S(2)}) %collective-permute-start) | collective-permute-done | bytes 294944 | tf_op jit(solution)/shard_map/while/body/eval_jaxpr/ppermute | solution.py:10
  188.9 3.7 collective-permute-done.1
  193.7 8.2 %collective-permute-done = bf16[128,1152]{1,0:T(8,128)(2,1)S(1)} collective-permute-done((bf16[128,1152]{1,0:T(8,128)(2,1)S(1)}, bf16[128,1152]{1,0:T(8,128)(2,1)S(1)}, u32[]{:S(2)}, u32[]{:S(2)}) %collective-permute-start) | collective-permute-done | bytes 294944 | tf_op jit(solution)/shard_map/while/body/eval_jaxpr/ppermute | solution.py:10
  204.4 3.7 collective-permute-done.1
  209.2 8.2 %collective-permute-done = bf16[128,1152]{1,0:T(8,128)(2,1)S(1)} collective-permute-done((bf16[128,1152]{1,0:T(8,128)(2,1)S(1)}, bf16[128,1152]{1,0:T(8,128)(2,1)S(1)}, u32[]{:S(2)}, u32[]{:S(2)}) %collective-permute-start) | collective-permute-done | bytes 294944 | tf_op jit(solution)/shard_map/while/body/eval_jaxpr/ppermute | solution.py:10
  220.0 3.7 collective-permute-done.1
  224.8 8.2 %collective-permute-done = bf16[128,1152]{1,0:T(8,128)(2,1)S(1)} collective-permute-done((bf16[128,1152]{1,0:T(8,128)(2,1)S(1)}, bf16[128,1152]{1,0:T(8,128)(2,1)S(1)}, u32[]{:S(2)}, u32[]{:S(2)}) %collective-permute-start) | collective-permute-done | bytes 294944 | tf_op jit(solution)/shard_map/while/body/eval_jaxpr/ppermute | solution.py:10
  240.3 8.2 %collective-permute-done = bf16[128,1152]{1,0:T(8,128)(2,1)S(1)} collective-permute-done((bf16[128,1152]{1,0:T(8,128)(2,1)S(1)}, bf16[128,1152]{1,0:T(8,128)(2,1)S(1)}, u32[]{:S(2)}, u32[]{:S(2)}) %collective-permute-start) | collective-permute-done | bytes 294944 | tf_op jit(solution)/shard_map/while/body/eval_jaxpr/ppermute | solution.py:10
  251.1 3.7 collective-permute-done.1
  255.9 8.2 %collective-permute-done = bf16[128,1152]{1,0:T(8,128)(2,1)S(1)} collective-permute-done((bf16[128,1152]{1,0:T(8,128)(2,1)S(1)}, bf16[128,1152]{1,0:T(8,128)(2,1)S(1)}, u32[]{:S(2)}, u32[]{:S(2)}) %collective-permute-start) | collective-permute-done | bytes 294944 | tf_op jit(solution)/shard_map/while/body/eval_jaxpr/ppermute | solution.py:10
  271.5 8.2 %collective-permute-done = bf16[128,1152]{1,0:T(8,128)(2,1)S(1)} collective-permute-done((bf16[128,1152]{1,0:T(8,128)(2,1)S(1)}, bf16[128,1152]{1,0:T(8,128)(2,1)S(1)}, u32[]{:S(2)}, u32[]{:S(2)}) %collective-permute-start) | collective-permute-done | bytes 294944 | tf_op jit(solution)/shard_map/while/body/eval_jaxpr/ppermute | solution.py:10
  287.0 8.2 %collective-permute-done = bf16[128,1152]{1,0:T(8,128)(2,1)S(1)} collective-permute-done((bf16[128,1152]{1,0:T(8,128)(2,1)S(1)}, bf16[128,1152]{1,0:T(8,128)(2,1)S(1)}, u32[]{:S(2)}, u32[]{:S(2)}) %collective-permute-start) | collective-permute-done | bytes 294944 | tf_op jit(solution)/shard_map/while/body/eval_jaxpr/ppermute | solution.py:10
  302.6 8.2 %collective-permute-done = bf16[128,1152]{1,0:T(8,128)(2,1)S(1)} collective-permute-done((bf16[128,1152]{1,0:T(8,128)(2,1)S(1)}, bf16[128,1152]{1,0:T(8,128)(2,1)S(1)}, u32[]{:S(2)}, u32[]{:S(2)}) %collective-permute-start) | collective-permute-done | bytes 294944 | tf_op jit(solution)/shard_map/while/body/eval_jaxpr/ppermute | solution.py:10
  318.1 8.2 %collective-permute-done = bf16[128,1152]{1,0:T(8,128)(2,1)S(1)} collective-permute-done((bf16[128,1152]{1,0:T(8,128)(2,1)S(1)}, bf16[128,1152]{1,0:T(8,128)(2,1)S(1)}, u32[]{:S(2)}, u32[]{:S(2)}) %collective-permute-start) | collective-permute-done | bytes 294944 | tf_op jit(solution)/shard_map/while/body/eval_jaxpr/ppermute | solution.py:10
  333.7 8.2 %collective-permute-done = bf16[128,1152]{1,0:T(8,128)(2,1)S(1)} collective-permute-done((bf16[128,1152]{1,0:T(8,128)(2,1)S(1)}, bf16[128,1152]{1,0:T(8,128)(2,1)S(1)}, u32[]{:S(2)}, u32[]{:S(2)}) %collective-permute-start) | collective-permute-done | bytes 294944 | tf_op jit(solution)/shard_map/while/body/eval_jaxpr/ppermute | solution.py:10
  349.2 8.2 %collective-permute-done = bf16[128,1152]{1,0:T(8,128)(2,1)S(1)} collective-permute-done((bf16[128,1152]{1,0:T(8,128)(2,1)S(1)}, bf16[128,1152]{1,0:T(8,128)(2,1)S(1)}, u32[]{:S(2)}, u32[]{:S(2)}) %collective-permute-start) | collective-permute-done | bytes 294944 | tf_op jit(solution)/shard_map/while/body/eval_jaxpr/ppermute | solution.py:10
  364.8 8.2 %collective-permute-done = bf16[128,1152]{1,0:T(8,128)(2,1)S(1)} collective-permute-done((bf16[128,1152]{1,0:T(8,128)(2,1)S(1)}, bf16[128,1152]{1,0:T(8,128)(2,1)S(1)}, u32[]{:S(2)}, u32[]{:S(2)}) %collective-permute-start) | collective-permute-done | bytes 294944 | tf_op jit(solution)/shard_map/while/body/eval_jaxpr/ppermute | solution.py:10
  380.3 8.2 %collective-permute-done = bf16[128,1152]{1,0:T(8,128)(2,1)S(1)} collective-permute-done((bf16[128,1152]{1,0:T(8,128)(2,1)S(1)}, bf16[128,1152]{1,0:T(8,128)(2,1)S(1)}, u32[]{:S(2)}, u32[]{:S(2)}) %collective-permute-start) | collective-permute-done | bytes 294944 | tf_op jit(solution)/shard_map/while/body/eval_jaxpr/ppermute | solution.py:10
  395.9 8.2 %collective-permute-done = bf16[128,1152]{1,0:T(8,128)(2,1)S(1)} collective-permute-done((bf16[128,1152]{1,0:T(8,128)(2,1)S(1)}, bf16[128,1152]{1,0:T(8,128)(2,1)S(1)}, u32[]{:S(2)}, u32[]{:S(2)}) %collective-permute-start) | collective-permute-done | bytes 294944 | tf_op jit(solution)/shard_map/while/body/eval_jaxpr/ppermute | solution.py:10
  411.4 8.2 %collective-permute-done = bf16[128,1152]{1,0:T(8,128)(2,1)S(1)} collective-permute-done((bf16[128,1152]{1,0:T(8,128)(2,1)S(1)}, bf16[128,1152]{1,0:T(8,128)(2,1)S(1)}, u32[]{:S(2)}, u32[]{:S(2)}) %collective-permute-start) | collective-permute-done | bytes 294944 | tf_op jit(solution)/shard_map/while/body/eval_jaxpr/ppermute | solution.py:10
  427.0 8.2 %collective-permute-done = bf16[128,1152]{1,0:T(8,128)(2,1)S(1)} collective-permute-done((bf16[128,1152]{1,0:T(8,128)(2,1)S(1)}, bf16[128,1152]{1,0:T(8,128)(2,1)S(1)}, u32[]{:S(2)}, u32[]{:S(2)}) %collective-permute-start) | collective-permute-done | bytes 294944 | tf_op jit(solution)/shard_map/while/body/eval_jaxpr/ppermute | solution.py:10
  442.5 8.2 %collective-permute-done = bf16[128,1152]{1,0:T(8,128)(2,1)S(1)} collective-permute-done((bf16[128,1152]{1,0:T(8,128)(2,1)S(1)}, bf16[128,1152]{1,0:T(8,128)(2,1)S(1)}, u32[]{:S(2)}, u32[]{:S(2)}) %collective-permute-start) | collective-permute-done | bytes 294944 | tf_op jit(solution)/shard_map/while/body/eval_jaxpr/ppermute | solution.py:10
  458.1 8.2 %collective-permute-done = bf16[128,1152]{1,0:T(8,128)(2,1)S(1)} collective-permute-done((bf16[128,1152]{1,0:T(8,128)(2,1)S(1)}, bf16[128,1152]{1,0:T(8,128)(2,1)S(1)}, u32[]{:S(2)}, u32[]{:S(2)}) %collective-permute-start) | collective-permute-done | bytes 294944 | tf_op jit(solution)/shard_map/while/body/eval_jaxpr/ppermute | solution.py:10
  473.7 8.2 %collective-permute-done = bf16[128,1152]{1,0:T(8,128)(2,1)S(1)} collective-permute-done((bf16[128,1152]{1,0:T(8,128)(2,1)S(1)}, bf16[128,1152]{1,0:T(8,128)(2,1)S(1)}, u32[]{:S(2)}, u32[]{:S(2)}) %collective-permute-start) | collective-permute-done | bytes 294944 | tf_op jit(solution)/shard_map/while/body/eval_jaxpr/ppermute | solution.py:10
  490.8 10.2 %collective-permute-done.2 = f32[128,1152]{1,0:T(8,128)S(1)} collective-permute-done((f32[128,1152]{1,0:T(8,128)S(1)}, f32[128,1152]{1,0:T(8,128)S(1)}, u32[]{:S(2)}, u32[]{:S(2)}) %collective-permute-start.2) | collective-permute-done | bytes 589856 | tf_op jit(solution)/shard_map/ppermute | solution.py:10
  (252 shorter events, 178.5 us)
Async XLA Ops:
  4.4 10.8 %collective-permute-start = (bf16[128,1152]{1,0:T(8,128)(2,1)S(1)}, bf16[128,1152]{1,0:T(8,128)(2,1)S(1)}, u32[]{:S(2)}, u32[]{:S(2)}) collective-permute-start(bf16[128,1152]{1,0:T(8,128)(2,1)S(1)} %get-tuple-element.137), channel_id=1, source_target_pairs={{248,0},{0,8},{8,16},{16,24},{24,32},{32,40},{40,48},{48,56},{56,6... | collective-permute-start | bytes 884744 | tf_op jit(solution)/shard_map/while/body/eval_jaxpr/ppermute | solution.py:10
  4.5 17.0 %collective-permute-start.1 = (f32[128,1152]{1,0:T(8,128)S(1)}, f32[128,1152]{1,0:T(8,128)S(1)}, u32[]{:S(2)}, u32[]{:S(2)}) collective-permute-start(f32[128,1152]{1,0:T(8,128)S(1)} %get-tuple-element.138), channel_id=1, source_target_pairs={{248,0},{0,8},{8,16},{16,24},{24,32},{32,40},{40,48},{48,56},{56,6... | collective-permute-start | bytes 1769480 | tf_op jit(solution)/shard_map/while/body/eval_jaxpr/ppermute | solution.py:10
  22.4 8.3 %collective-permute-start = (bf16[128,1152]{1,0:T(8,128)(2,1)S(1)}, bf16[128,1152]{1,0:T(8,128)(2,1)S(1)}, u32[]{:S(2)}, u32[]{:S(2)}) collective-permute-start(bf16[128,1152]{1,0:T(8,128)(2,1)S(1)} %get-tuple-element.137), channel_id=1, source_target_pairs={{248,0},{0,8},{8,16},{16,24},{24,32},{32,40},{40,48},{48,56},{56,6... | collective-permute-start | bytes 884744 | tf_op jit(solution)/shard_map/while/body/eval_jaxpr/ppermute | solution.py:10
  22.5 14.6 %collective-permute-start.1 = (f32[128,1152]{1,0:T(8,128)S(1)}, f32[128,1152]{1,0:T(8,128)S(1)}, u32[]{:S(2)}, u32[]{:S(2)}) collective-permute-start(f32[128,1152]{1,0:T(8,128)S(1)} %get-tuple-element.138), channel_id=1, source_target_pairs={{248,0},{0,8},{8,16},{16,24},{24,32},{32,40},{40,48},{48,56},{56,6... | collective-permute-start | bytes 1769480 | tf_op jit(solution)/shard_map/while/body/eval_jaxpr/ppermute | solution.py:10
  38.0 8.3 %collective-permute-start = (bf16[128,1152]{1,0:T(8,128)(2,1)S(1)}, bf16[128,1152]{1,0:T(8,128)(2,1)S(1)}, u32[]{:S(2)}, u32[]{:S(2)}) collective-permute-start(bf16[128,1152]{1,0:T(8,128)(2,1)S(1)} %get-tuple-element.137), channel_id=1, source_target_pairs={{248,0},{0,8},{8,16},{16,24},{24,32},{32,40},{40,48},{48,56},{56,6... | collective-permute-start | bytes 884744 | tf_op jit(solution)/shard_map/while/body/eval_jaxpr/ppermute | solution.py:10
  38.1 14.6 %collective-permute-start.1 = (f32[128,1152]{1,0:T(8,128)S(1)}, f32[128,1152]{1,0:T(8,128)S(1)}, u32[]{:S(2)}, u32[]{:S(2)}) collective-permute-start(f32[128,1152]{1,0:T(8,128)S(1)} %get-tuple-element.138), channel_id=1, source_target_pairs={{248,0},{0,8},{8,16},{16,24},{24,32},{32,40},{40,48},{48,56},{56,6... | collective-permute-start | bytes 1769480 | tf_op jit(solution)/shard_map/while/body/eval_jaxpr/ppermute | solution.py:10
  53.5 8.3 %collective-permute-start = (bf16[128,1152]{1,0:T(8,128)(2,1)S(1)}, bf16[128,1152]{1,0:T(8,128)(2,1)S(1)}, u32[]{:S(2)}, u32[]{:S(2)}) collective-permute-start(bf16[128,1152]{1,0:T(8,128)(2,1)S(1)} %get-tuple-element.137), channel_id=1, source_target_pairs={{248,0},{0,8},{8,16},{16,24},{24,32},{32,40},{40,48},{48,56},{56,6... | collective-permute-start | bytes 884744 | tf_op jit(solution)/shard_map/while/body/eval_jaxpr/ppermute | solution.py:10
  53.6 14.6 %collective-permute-start.1 = (f32[128,1152]{1,0:T(8,128)S(1)}, f32[128,1152]{1,0:T(8,128)S(1)}, u32[]{:S(2)}, u32[]{:S(2)}) collective-permute-start(f32[128,1152]{1,0:T(8,128)S(1)} %get-tuple-element.138), channel_id=1, source_target_pairs={{248,0},{0,8},{8,16},{16,24},{24,32},{32,40},{40,48},{48,56},{56,6... | collective-permute-start | bytes 1769480 | tf_op jit(solution)/shard_map/while/body/eval_jaxpr/ppermute | solution.py:10
  69.1 8.3 %collective-permute-start = (bf16[128,1152]{1,0:T(8,128)(2,1)S(1)}, bf16[128,1152]{1,0:T(8,128)(2,1)S(1)}, u32[]{:S(2)}, u32[]{:S(2)}) collective-permute-start(bf16[128,1152]{1,0:T(8,128)(2,1)S(1)} %get-tuple-element.137), channel_id=1, source_target_pairs={{248,0},{0,8},{8,16},{16,24},{24,32},{32,40},{40,48},{48,56},{56,6... | collective-permute-start | bytes 884744 | tf_op jit(solution)/shard_map/while/body/eval_jaxpr/ppermute | solution.py:10
  69.2 14.6 %collective-permute-start.1 = (f32[128,1152]{1,0:T(8,128)S(1)}, f32[128,1152]{1,0:T(8,128)S(1)}, u32[]{:S(2)}, u32[]{:S(2)}) collective-permute-start(f32[128,1152]{1,0:T(8,128)S(1)} %get-tuple-element.138), channel_id=1, source_target_pairs={{248,0},{0,8},{8,16},{16,24},{24,32},{32,40},{40,48},{48,56},{56,6... | collective-permute-start | bytes 1769480 | tf_op jit(solution)/shard_map/while/body/eval_jaxpr/ppermute | solution.py:10
  84.6 8.3 %collective-permute-start = (bf16[128,1152]{1,0:T(8,128)(2,1)S(1)}, bf16[128,1152]{1,0:T(8,128)(2,1)S(1)}, u32[]{:S(2)}, u32[]{:S(2)}) collective-permute-start(bf16[128,1152]{1,0:T(8,128)(2,1)S(1)} %get-tuple-element.137), channel_id=1, source_target_pairs={{248,0},{0,8},{8,16},{16,24},{24,32},{32,40},{40,48},{48,56},{56,6... | collective-permute-start | bytes 884744 | tf_op jit(solution)/shard_map/while/body/eval_jaxpr/ppermute | solution.py:10
  84.7 14.6 %collective-permute-start.1 = (f32[128,1152]{1,0:T(8,128)S(1)}, f32[128,1152]{1,0:T(8,128)S(1)}, u32[]{:S(2)}, u32[]{:S(2)}) collective-permute-start(f32[128,1152]{1,0:T(8,128)S(1)} %get-tuple-element.138), channel_id=1, source_target_pairs={{248,0},{0,8},{8,16},{16,24},{24,32},{32,40},{40,48},{48,56},{56,6... | collective-permute-start | bytes 1769480 | tf_op jit(solution)/shard_map/while/body/eval_jaxpr/ppermute | solution.py:10
  100.2 8.3 %collective-permute-start = (bf16[128,1152]{1,0:T(8,128)(2,1)S(1)}, bf16[128,1152]{1,0:T(8,128)(2,1)S(1)}, u32[]{:S(2)}, u32[]{:S(2)}) collective-permute-start(bf16[128,1152]{1,0:T(8,128)(2,1)S(1)} %get-tuple-element.137), channel_id=1, source_target_pairs={{248,0},{0,8},{8,16},{16,24},{24,32},{32,40},{40,48},{48,56},{56,6... | collective-permute-start | bytes 884744 | tf_op jit(solution)/shard_map/while/body/eval_jaxpr/ppermute | solution.py:10
  100.3 14.6 %collective-permute-start.1 = (f32[128,1152]{1,0:T(8,128)S(1)}, f32[128,1152]{1,0:T(8,128)S(1)}, u32[]{:S(2)}, u32[]{:S(2)}) collective-permute-start(f32[128,1152]{1,0:T(8,128)S(1)} %get-tuple-element.138), channel_id=1, source_target_pairs={{248,0},{0,8},{8,16},{16,24},{24,32},{32,40},{40,48},{48,56},{56,6... | collective-permute-start | bytes 1769480 | tf_op jit(solution)/shard_map/while/body/eval_jaxpr/ppermute | solution.py:10
  115.7 8.3 %collective-permute-start = (bf16[128,1152]{1,0:T(8,128)(2,1)S(1)}, bf16[128,1152]{1,0:T(8,128)(2,1)S(1)}, u32[]{:S(2)}, u32[]{:S(2)}) collective-permute-start(bf16[128,1152]{1,0:T(8,128)(2,1)S(1)} %get-tuple-element.137), channel_id=1, source_target_pairs={{248,0},{0,8},{8,16},{16,24},{24,32},{32,40},{40,48},{48,56},{56,6... | collective-permute-start | bytes 884744 | tf_op jit(solution)/shard_map/while/body/eval_jaxpr/ppermute | solution.py:10
  115.8 14.6 %collective-permute-start.1 = (f32[128,1152]{1,0:T(8,128)S(1)}, f32[128,1152]{1,0:T(8,128)S(1)}, u32[]{:S(2)}, u32[]{:S(2)}) collective-permute-start(f32[128,1152]{1,0:T(8,128)S(1)} %get-tuple-element.138), channel_id=1, source_target_pairs={{248,0},{0,8},{8,16},{16,24},{24,32},{32,40},{40,48},{48,56},{56,6... | collective-permute-start | bytes 1769480 | tf_op jit(solution)/shard_map/while/body/eval_jaxpr/ppermute | solution.py:10
  131.3 8.3 %collective-permute-start = (bf16[128,1152]{1,0:T(8,128)(2,1)S(1)}, bf16[128,1152]{1,0:T(8,128)(2,1)S(1)}, u32[]{:S(2)}, u32[]{:S(2)}) collective-permute-start(bf16[128,1152]{1,0:T(8,128)(2,1)S(1)} %get-tuple-element.137), channel_id=1, source_target_pairs={{248,0},{0,8},{8,16},{16,24},{24,32},{32,40},{40,48},{48,56},{56,6... | collective-permute-start | bytes 884744 | tf_op jit(solution)/shard_map/while/body/eval_jaxpr/ppermute | solution.py:10
  131.4 14.6 %collective-permute-start.1 = (f32[128,1152]{1,0:T(8,128)S(1)}, f32[128,1152]{1,0:T(8,128)S(1)}, u32[]{:S(2)}, u32[]{:S(2)}) collective-permute-start(f32[128,1152]{1,0:T(8,128)S(1)} %get-tuple-element.138), channel_id=1, source_target_pairs={{248,0},{0,8},{8,16},{16,24},{24,32},{32,40},{40,48},{48,56},{56,6... | collective-permute-start | bytes 1769480 | tf_op jit(solution)/shard_map/while/body/eval_jaxpr/ppermute | solution.py:10
  146.8 8.3 %collective-permute-start = (bf16[128,1152]{1,0:T(8,128)(2,1)S(1)}, bf16[128,1152]{1,0:T(8,128)(2,1)S(1)}, u32[]{:S(2)}, u32[]{:S(2)}) collective-permute-start(bf16[128,1152]{1,0:T(8,128)(2,1)S(1)} %get-tuple-element.137), channel_id=1, source_target_pairs={{248,0},{0,8},{8,16},{16,24},{24,32},{32,40},{40,48},{48,56},{56,6... | collective-permute-start | bytes 884744 | tf_op jit(solution)/shard_map/while/body/eval_jaxpr/ppermute | solution.py:10
  146.9 14.6 %collective-permute-start.1 = (f32[128,1152]{1,0:T(8,128)S(1)}, f32[128,1152]{1,0:T(8,128)S(1)}, u32[]{:S(2)}, u32[]{:S(2)}) collective-permute-start(f32[128,1152]{1,0:T(8,128)S(1)} %get-tuple-element.138), channel_id=1, source_target_pairs={{248,0},{0,8},{8,16},{16,24},{24,32},{32,40},{40,48},{48,56},{56,6... | collective-permute-start | bytes 1769480 | tf_op jit(solution)/shard_map/while/body/eval_jaxpr/ppermute | solution.py:10
  162.4 8.3 %collective-permute-start = (bf16[128,1152]{1,0:T(8,128)(2,1)S(1)}, bf16[128,1152]{1,0:T(8,128)(2,1)S(1)}, u32[]{:S(2)}, u32[]{:S(2)}) collective-permute-start(bf16[128,1152]{1,0:T(8,128)(2,1)S(1)} %get-tuple-element.137), channel_id=1, source_target_pairs={{248,0},{0,8},{8,16},{16,24},{24,32},{32,40},{40,48},{48,56},{56,6... | collective-permute-start | bytes 884744 | tf_op jit(solution)/shard_map/while/body/eval_jaxpr/ppermute | solution.py:10
  162.5 14.6 %collective-permute-start.1 = (f32[128,1152]{1,0:T(8,128)S(1)}, f32[128,1152]{1,0:T(8,128)S(1)}, u32[]{:S(2)}, u32[]{:S(2)}) collective-permute-start(f32[128,1152]{1,0:T(8,128)S(1)} %get-tuple-element.138), channel_id=1, source_target_pairs={{248,0},{0,8},{8,16},{16,24},{24,32},{32,40},{40,48},{48,56},{56,6... | collective-permute-start | bytes 1769480 | tf_op jit(solution)/shard_map/while/body/eval_jaxpr/ppermute | solution.py:10
  178.0 8.3 %collective-permute-start = (bf16[128,1152]{1,0:T(8,128)(2,1)S(1)}, bf16[128,1152]{1,0:T(8,128)(2,1)S(1)}, u32[]{:S(2)}, u32[]{:S(2)}) collective-permute-start(bf16[128,1152]{1,0:T(8,128)(2,1)S(1)} %get-tuple-element.137), channel_id=1, source_target_pairs={{248,0},{0,8},{8,16},{16,24},{24,32},{32,40},{40,48},{48,56},{56,6... | collective-permute-start | bytes 884744 | tf_op jit(solution)/shard_map/while/body/eval_jaxpr/ppermute | solution.py:10
  178.0 14.6 %collective-permute-start.1 = (f32[128,1152]{1,0:T(8,128)S(1)}, f32[128,1152]{1,0:T(8,128)S(1)}, u32[]{:S(2)}, u32[]{:S(2)}) collective-permute-start(f32[128,1152]{1,0:T(8,128)S(1)} %get-tuple-element.138), channel_id=1, source_target_pairs={{248,0},{0,8},{8,16},{16,24},{24,32},{32,40},{40,48},{48,56},{56,6... | collective-permute-start | bytes 1769480 | tf_op jit(solution)/shard_map/while/body/eval_jaxpr/ppermute | solution.py:10
  193.5 8.3 %collective-permute-start = (bf16[128,1152]{1,0:T(8,128)(2,1)S(1)}, bf16[128,1152]{1,0:T(8,128)(2,1)S(1)}, u32[]{:S(2)}, u32[]{:S(2)}) collective-permute-start(bf16[128,1152]{1,0:T(8,128)(2,1)S(1)} %get-tuple-element.137), channel_id=1, source_target_pairs={{248,0},{0,8},{8,16},{16,24},{24,32},{32,40},{40,48},{48,56},{56,6... | collective-permute-start | bytes 884744 | tf_op jit(solution)/shard_map/while/body/eval_jaxpr/ppermute | solution.py:10
  193.6 14.6 %collective-permute-start.1 = (f32[128,1152]{1,0:T(8,128)S(1)}, f32[128,1152]{1,0:T(8,128)S(1)}, u32[]{:S(2)}, u32[]{:S(2)}) collective-permute-start(f32[128,1152]{1,0:T(8,128)S(1)} %get-tuple-element.138), channel_id=1, source_target_pairs={{248,0},{0,8},{8,16},{16,24},{24,32},{32,40},{40,48},{48,56},{56,6... | collective-permute-start | bytes 1769480 | tf_op jit(solution)/shard_map/while/body/eval_jaxpr/ppermute | solution.py:10
  209.2 14.6 %collective-permute-start.1 = (f32[128,1152]{1,0:T(8,128)S(1)}, f32[128,1152]{1,0:T(8,128)S(1)}, u32[]{:S(2)}, u32[]{:S(2)}) collective-permute-start(f32[128,1152]{1,0:T(8,128)S(1)} %get-tuple-element.138), channel_id=1, source_target_pairs={{248,0},{0,8},{8,16},{16,24},{24,32},{32,40},{40,48},{48,56},{56,6... | collective-permute-start | bytes 1769480 | tf_op jit(solution)/shard_map/while/body/eval_jaxpr/ppermute | solution.py:10
  224.7 14.6 %collective-permute-start.1 = (f32[128,1152]{1,0:T(8,128)S(1)}, f32[128,1152]{1,0:T(8,128)S(1)}, u32[]{:S(2)}, u32[]{:S(2)}) collective-permute-start(f32[128,1152]{1,0:T(8,128)S(1)} %get-tuple-element.138), channel_id=1, source_target_pairs={{248,0},{0,8},{8,16},{16,24},{24,32},{32,40},{40,48},{48,56},{56,6... | collective-permute-start | bytes 1769480 | tf_op jit(solution)/shard_map/while/body/eval_jaxpr/ppermute | solution.py:10
  240.3 14.6 %collective-permute-start.1 = (f32[128,1152]{1,0:T(8,128)S(1)}, f32[128,1152]{1,0:T(8,128)S(1)}, u32[]{:S(2)}, u32[]{:S(2)}) collective-permute-start(f32[128,1152]{1,0:T(8,128)S(1)} %get-tuple-element.138), channel_id=1, source_target_pairs={{248,0},{0,8},{8,16},{16,24},{24,32},{32,40},{40,48},{48,56},{56,6... | collective-permute-start | bytes 1769480 | tf_op jit(solution)/shard_map/while/body/eval_jaxpr/ppermute | solution.py:10
  255.8 14.6 %collective-permute-start.1 = (f32[128,1152]{1,0:T(8,128)S(1)}, f32[128,1152]{1,0:T(8,128)S(1)}, u32[]{:S(2)}, u32[]{:S(2)}) collective-permute-start(f32[128,1152]{1,0:T(8,128)S(1)} %get-tuple-element.138), channel_id=1, source_target_pairs={{248,0},{0,8},{8,16},{16,24},{24,32},{32,40},{40,48},{48,56},{56,6... | collective-permute-start | bytes 1769480 | tf_op jit(solution)/shard_map/while/body/eval_jaxpr/ppermute | solution.py:10
  271.4 14.6 %collective-permute-start.1 = (f32[128,1152]{1,0:T(8,128)S(1)}, f32[128,1152]{1,0:T(8,128)S(1)}, u32[]{:S(2)}, u32[]{:S(2)}) collective-permute-start(f32[128,1152]{1,0:T(8,128)S(1)} %get-tuple-element.138), channel_id=1, source_target_pairs={{248,0},{0,8},{8,16},{16,24},{24,32},{32,40},{40,48},{48,56},{56,6... | collective-permute-start | bytes 1769480 | tf_op jit(solution)/shard_map/while/body/eval_jaxpr/ppermute | solution.py:10
  286.9 14.6 %collective-permute-start.1 = (f32[128,1152]{1,0:T(8,128)S(1)}, f32[128,1152]{1,0:T(8,128)S(1)}, u32[]{:S(2)}, u32[]{:S(2)}) collective-permute-start(f32[128,1152]{1,0:T(8,128)S(1)} %get-tuple-element.138), channel_id=1, source_target_pairs={{248,0},{0,8},{8,16},{16,24},{24,32},{32,40},{40,48},{48,56},{56,6... | collective-permute-start | bytes 1769480 | tf_op jit(solution)/shard_map/while/body/eval_jaxpr/ppermute | solution.py:10
  302.4 8.3 %collective-permute-start = (bf16[128,1152]{1,0:T(8,128)(2,1)S(1)}, bf16[128,1152]{1,0:T(8,128)(2,1)S(1)}, u32[]{:S(2)}, u32[]{:S(2)}) collective-permute-start(bf16[128,1152]{1,0:T(8,128)(2,1)S(1)} %get-tuple-element.137), channel_id=1, source_target_pairs={{248,0},{0,8},{8,16},{16,24},{24,32},{32,40},{40,48},{48,56},{56,6... | collective-permute-start | bytes 884744 | tf_op jit(solution)/shard_map/while/body/eval_jaxpr/ppermute | solution.py:10
  302.5 14.6 %collective-permute-start.1 = (f32[128,1152]{1,0:T(8,128)S(1)}, f32[128,1152]{1,0:T(8,128)S(1)}, u32[]{:S(2)}, u32[]{:S(2)}) collective-permute-start(f32[128,1152]{1,0:T(8,128)S(1)} %get-tuple-element.138), channel_id=1, source_target_pairs={{248,0},{0,8},{8,16},{16,24},{24,32},{32,40},{40,48},{48,56},{56,6... | collective-permute-start | bytes 1769480 | tf_op jit(solution)/shard_map/while/body/eval_jaxpr/ppermute | solution.py:10
  318.0 14.6 %collective-permute-start.1 = (f32[128,1152]{1,0:T(8,128)S(1)}, f32[128,1152]{1,0:T(8,128)S(1)}, u32[]{:S(2)}, u32[]{:S(2)}) collective-permute-start(f32[128,1152]{1,0:T(8,128)S(1)} %get-tuple-element.138), channel_id=1, source_target_pairs={{248,0},{0,8},{8,16},{16,24},{24,32},{32,40},{40,48},{48,56},{56,6... | collective-permute-start | bytes 1769480 | tf_op jit(solution)/shard_map/while/body/eval_jaxpr/ppermute | solution.py:10
  333.6 14.6 %collective-permute-start.1 = (f32[128,1152]{1,0:T(8,128)S(1)}, f32[128,1152]{1,0:T(8,128)S(1)}, u32[]{:S(2)}, u32[]{:S(2)}) collective-permute-start(f32[128,1152]{1,0:T(8,128)S(1)} %get-tuple-element.138), channel_id=1, source_target_pairs={{248,0},{0,8},{8,16},{16,24},{24,32},{32,40},{40,48},{48,56},{56,6... | collective-permute-start | bytes 1769480 | tf_op jit(solution)/shard_map/while/body/eval_jaxpr/ppermute | solution.py:10
  349.1 14.6 %collective-permute-start.1 = (f32[128,1152]{1,0:T(8,128)S(1)}, f32[128,1152]{1,0:T(8,128)S(1)}, u32[]{:S(2)}, u32[]{:S(2)}) collective-permute-start(f32[128,1152]{1,0:T(8,128)S(1)} %get-tuple-element.138), channel_id=1, source_target_pairs={{248,0},{0,8},{8,16},{16,24},{24,32},{32,40},{40,48},{48,56},{56,6... | collective-permute-start | bytes 1769480 | tf_op jit(solution)/shard_map/while/body/eval_jaxpr/ppermute | solution.py:10
  364.7 14.6 %collective-permute-start.1 = (f32[128,1152]{1,0:T(8,128)S(1)}, f32[128,1152]{1,0:T(8,128)S(1)}, u32[]{:S(2)}, u32[]{:S(2)}) collective-permute-start(f32[128,1152]{1,0:T(8,128)S(1)} %get-tuple-element.138), channel_id=1, source_target_pairs={{248,0},{0,8},{8,16},{16,24},{24,32},{32,40},{40,48},{48,56},{56,6... | collective-permute-start | bytes 1769480 | tf_op jit(solution)/shard_map/while/body/eval_jaxpr/ppermute | solution.py:10
  380.2 8.3 %collective-permute-start = (bf16[128,1152]{1,0:T(8,128)(2,1)S(1)}, bf16[128,1152]{1,0:T(8,128)(2,1)S(1)}, u32[]{:S(2)}, u32[]{:S(2)}) collective-permute-start(bf16[128,1152]{1,0:T(8,128)(2,1)S(1)} %get-tuple-element.137), channel_id=1, source_target_pairs={{248,0},{0,8},{8,16},{16,24},{24,32},{32,40},{40,48},{48,56},{56,6... | collective-permute-start | bytes 884744 | tf_op jit(solution)/shard_map/while/body/eval_jaxpr/ppermute | solution.py:10
  380.2 14.6 %collective-permute-start.1 = (f32[128,1152]{1,0:T(8,128)S(1)}, f32[128,1152]{1,0:T(8,128)S(1)}, u32[]{:S(2)}, u32[]{:S(2)}) collective-permute-start(f32[128,1152]{1,0:T(8,128)S(1)} %get-tuple-element.138), channel_id=1, source_target_pairs={{248,0},{0,8},{8,16},{16,24},{24,32},{32,40},{40,48},{48,56},{56,6... | collective-permute-start | bytes 1769480 | tf_op jit(solution)/shard_map/while/body/eval_jaxpr/ppermute | solution.py:10
  395.8 14.6 %collective-permute-start.1 = (f32[128,1152]{1,0:T(8,128)S(1)}, f32[128,1152]{1,0:T(8,128)S(1)}, u32[]{:S(2)}, u32[]{:S(2)}) collective-permute-start(f32[128,1152]{1,0:T(8,128)S(1)} %get-tuple-element.138), channel_id=1, source_target_pairs={{248,0},{0,8},{8,16},{16,24},{24,32},{32,40},{40,48},{48,56},{56,6... | collective-permute-start | bytes 1769480 | tf_op jit(solution)/shard_map/while/body/eval_jaxpr/ppermute | solution.py:10
  411.3 14.6 %collective-permute-start.1 = (f32[128,1152]{1,0:T(8,128)S(1)}, f32[128,1152]{1,0:T(8,128)S(1)}, u32[]{:S(2)}, u32[]{:S(2)}) collective-permute-start(f32[128,1152]{1,0:T(8,128)S(1)} %get-tuple-element.138), channel_id=1, source_target_pairs={{248,0},{0,8},{8,16},{16,24},{24,32},{32,40},{40,48},{48,56},{56,6... | collective-permute-start | bytes 1769480 | tf_op jit(solution)/shard_map/while/body/eval_jaxpr/ppermute | solution.py:10
  426.9 14.6 %collective-permute-start.1 = (f32[128,1152]{1,0:T(8,128)S(1)}, f32[128,1152]{1,0:T(8,128)S(1)}, u32[]{:S(2)}, u32[]{:S(2)}) collective-permute-start(f32[128,1152]{1,0:T(8,128)S(1)} %get-tuple-element.138), channel_id=1, source_target_pairs={{248,0},{0,8},{8,16},{16,24},{24,32},{32,40},{40,48},{48,56},{56,6... | collective-permute-start | bytes 1769480 | tf_op jit(solution)/shard_map/while/body/eval_jaxpr/ppermute | solution.py:10
  442.5 14.6 %collective-permute-start.1 = (f32[128,1152]{1,0:T(8,128)S(1)}, f32[128,1152]{1,0:T(8,128)S(1)}, u32[]{:S(2)}, u32[]{:S(2)}) collective-permute-start(f32[128,1152]{1,0:T(8,128)S(1)} %get-tuple-element.138), channel_id=1, source_target_pairs={{248,0},{0,8},{8,16},{16,24},{24,32},{32,40},{40,48},{48,56},{56,6... | collective-permute-start | bytes 1769480 | tf_op jit(solution)/shard_map/while/body/eval_jaxpr/ppermute | solution.py:10
  457.9 8.3 %collective-permute-start = (bf16[128,1152]{1,0:T(8,128)(2,1)S(1)}, bf16[128,1152]{1,0:T(8,128)(2,1)S(1)}, u32[]{:S(2)}, u32[]{:S(2)}) collective-permute-start(bf16[128,1152]{1,0:T(8,128)(2,1)S(1)} %get-tuple-element.137), channel_id=1, source_target_pairs={{248,0},{0,8},{8,16},{16,24},{24,32},{32,40},{40,48},{48,56},{56,6... | collective-permute-start | bytes 884744 | tf_op jit(solution)/shard_map/while/body/eval_jaxpr/ppermute | solution.py:10
  458.0 14.6 %collective-permute-start.1 = (f32[128,1152]{1,0:T(8,128)S(1)}, f32[128,1152]{1,0:T(8,128)S(1)}, u32[]{:S(2)}, u32[]{:S(2)}) collective-permute-start(f32[128,1152]{1,0:T(8,128)S(1)} %get-tuple-element.138), channel_id=1, source_target_pairs={{248,0},{0,8},{8,16},{16,24},{24,32},{32,40},{40,48},{48,56},{56,6... | collective-permute-start | bytes 1769480 | tf_op jit(solution)/shard_map/while/body/eval_jaxpr/ppermute | solution.py:10
  473.6 14.6 %collective-permute-start.1 = (f32[128,1152]{1,0:T(8,128)S(1)}, f32[128,1152]{1,0:T(8,128)S(1)}, u32[]{:S(2)}, u32[]{:S(2)}) collective-permute-start(f32[128,1152]{1,0:T(8,128)S(1)} %get-tuple-element.138), channel_id=1, source_target_pairs={{248,0},{0,8},{8,16},{16,24},{24,32},{32,40},{40,48},{48,56},{56,6... | collective-permute-start | bytes 1769480 | tf_op jit(solution)/shard_map/while/body/eval_jaxpr/ppermute | solution.py:10
  489.5 11.4 %collective-permute-start.2 = (f32[128,1152]{1,0:T(8,128)S(1)}, f32[128,1152]{1,0:T(8,128)S(1)}, u32[]{:S(2)}, u32[]{:S(2)}) collective-permute-start(f32[128,1152]{1,0:T(8,128)S(1)} %get-tuple-element.49), channel_id=1, source_target_pairs={{248,0},{0,8},{8,16},{16,24},{24,32},{32,40},{40,48},{48,56},{56,6... | collective-permute-start | bytes 1769480 | tf_op jit(solution)/shard_map/ppermute | solution.py:10
  (18 other events, 129.4 us)
where the time goes:
time: 503 us; the launch traced here: 502 us
  waiting for transfers between devices  380 us (76%)
  matrix products  106 us (21%)
  starting transfers between devices  6.76 us (1%)
    ppermute x63, waiting for transfers between devices, from_behind(): return lax.ppermute(block, axis, route)  380 us
    dot_general x32, matrix products, score_tile(): lax.dot_general(images, texts, (((1,), (1,)), ((), ())), preferred_elemen...  49.8 us
    dot_general x32, matrix products, visit(): jnp.dot(coef, block, preferred_element_type=jnp.float32)  29.1 us
    dot_general x32, matrix products, visit(): lax.dot_general(coef, zi, (((0,), (0,)), ((), ())), preferred_element_typ...  27.4 us
  transfers between devices with their start and end apart: 63, of which 63 were waited for; matrix products, arithmetic and copies ran while one was open for 16% of the time, Pallas kernels for 0%

commit v1 on v0

v1 whole, which is shorter than its diff:
```python
import functools

import jax
import jax.numpy as jnp
from jax import lax
from jax.experimental import pallas as pl
from jax.experimental.pallas import tpu as pltpu
from jax.sharding import PartitionSpec as P

MESH = pl.DeviceIdType.MESH
F32 = jnp.float32
BF16 = jnp.bfloat16

RING = 8
QUAD = 4
RIGHT, LEFT = 0, 1
EPS = 1e-06
CODE = 2.0**13
TINY = 2.0**-126


def encode(x):
    a = x * CODE
    a2 = a * a
    return (a2 * a2 * a).astype(BF16)


def decode(y):
    y = y.astype(F32)
    root = jnp.exp(jnp.log(jnp.maximum(jnp.abs(y), TINY)) * 0.2) * (1.0 / CODE)
    return jnp.where(y < 0, -root, root)


def nt(a, b):
    return lax.dot_general(a, b, (((1,), (1,)), ((), ())), preferred_element_type=F32)


def tn(a, b):
    return lax.dot_general(a, b, (((0,), (0,)), ((), ())), preferred_element_type=F32)


def kernel(
    img_ref,
    txt_ref,
    scale_ref,
    bias_ref,
    loss_ref,
    gi_ref,
    gt_ref,
    img,
    txt,
    part,
    coefs,
    sums,
    rs_send,
    rs_recv,
    core_recv,
    y_recv,
    unit_i,
    unit_t,
    inv_i,
    inv_t,
    loss_part,
    loss_recv,
    ag_ssem,
    ag_rsem,
    rs_ssem,
    rs_rsem,
    loss_ssem,
    loss_rsem,
    t_ssem,
    t_rsem,
    c_ssem,
    c_rsem,
    y_ssem,
    y_rsem,
):
    rows = img_ref.shape[0]
    half = rows // 2
    sub = half // 2
    me = lax.axis_index("blk")
    n = RING * QUAD
    to = (lax.rem(me + QUAD, n), lax.rem(me + n - QUAD, n))
    other_core = me + 1 - 2 * lax.rem(me, 2)
    other_y = me + 2 - 4 * lax.rem(lax.div(me, 2), 2)

    def copy(src, dst, ssem, rsem, device):
        return pltpu.make_async_remote_copy(
            src_ref=src,
            dst_ref=dst,
            send_sem=ssem,
            recv_sem=rsem,
            device_id={"blk": device},
            device_id_type=MESH,
        )

    barrier = pltpu.get_barrier_semaphore()
    for peer in (*to, other_core, other_y):
        pl.semaphore_signal(barrier, inc=1, device_id={"blk": peer}, device_id_type=MESH)

    scale = scale_ref[0]
    bias = bias_ref[0]

    def normalize(src, at, size, unit, inv, out):
        values = src[pl.ds(at, size), :].astype(F32)
        norm = jnp.sqrt(jnp.sum(values * values, axis=1, keepdims=True) + EPS)
        inverse = 1.0 / norm
        u = values * inverse
        unit[pl.ds(at, size), :] = u
        inv[pl.ds(at, size), :] = jnp.broadcast_to(inverse, (size, 128))
        out[pl.ds(at, size), :] = u.astype(BF16)

    def gather(way, hop, piece):
        here = hop - 1 if way == RIGHT else lax.rem(RING + 1 - hop, RING)
        there = hop if way == RIGHT else RING - hop
        src = img.at[pl.ds(pl.multiple_of(here * rows + piece * half, half), half), :]
        dst = img.at[pl.ds(pl.multiple_of(there * rows + piece * half, half), half), :]
        at = (hop - 1) * 2 + piece
        return copy(src, dst, ag_ssem.at[way, at], ag_rsem.at[way, at], to[way])

    normalize(img_ref, 0, half, unit_i, inv_i, img)
    normalize(img_ref, half, half, unit_i, inv_i, img)
    pl.semaphore_wait(barrier, 4)
    gather(RIGHT, 1, 0).start()
    gather(LEFT, 1, 1).start()
    gather(RIGHT, 1, 1).start()
    gather(LEFT, 1, 0).start()

    normalize(txt_ref, 0, rows, unit_t, inv_t, txt)

    def text_copy(i):
        src = (0, 0, 2)[i]
        dst = (1, 2, 3)[i]
        device = (other_core, other_y, other_core)[i]
        return copy(
            txt.at[pl.ds(src * rows, rows), :],
            txt.at[pl.ds(dst * rows, rows), :],
            t_ssem.at[i],
            t_rsem.at[i],
            device,
        )

    text_copy(1).start()
    text_copy(0).start()

    def tile(slot, own):
        at = slot * rows if own else pl.multiple_of(slot * rows, rows)
        zi = img[pl.ds(at, rows), :]
        wide = 2 * rows
        total = jnp.zeros((rows, rows), F32)
        for h in range(2):
            m = nt(zi, txt[pl.ds(h * wide, wide), :]) * scale + bias
            if own and h == 0:
                eye = lax.broadcasted_iota(jnp.int32, m.shape, 0) == lax.broadcasted_iota(
                    jnp.int32, m.shape, 1
                )
                m = jnp.where(eye, -m, m)
            e = jnp.exp(-jnp.abs(m))
            soft = jnp.maximum(m, 0.0) + jnp.log1p(e)
            r = 1.0 / (1.0 + e)
            coef = jnp.where(m >= 0, r, e * r)
            if own and h == 0:
                coef = jnp.where(eye, -coef, coef)
            total = total + soft[:, :rows] + soft[:, rows:]
            coefs[pl.ds(at, rows), pl.ds(h * wide, wide)] = coef.astype(BF16)
        part[slot] = jnp.dot(coefs[pl.ds(at, rows), :], txt[...], preferred_element_type=F32)
        across = jnp.sum(total.T, axis=0, keepdims=True)
        loss_part[slot] = jnp.broadcast_to(across, (8, rows))

    def arrive(hop):
        for first in (True, False):
            for way in (RIGHT, LEFT):
                piece = (0 if first else 1) if way == RIGHT else (1 if first else 0)
                gather(way, hop, piece).wait_recv()
                if first:
                    gather(way, hop + 1, piece).start()
                else:

                    @pl.when(hop < 3)
                    def _():
                        gather(way, hop + 1, piece).start()

    def chunk(way, idx, s):
        src = rs_send.at[way, idx, pl.ds(pl.multiple_of(s * sub, sub), sub), :]
        dst = rs_recv.at[way, idx, pl.ds(pl.multiple_of(s * sub, sub), sub), :]
        at = idx * 2 + s
        return copy(src, dst, rs_ssem.at[way, at], rs_rsem.at[way, at], to[way])

    def late(way, j):
        slot = 4 + j if way == RIGHT else 4 - j
        return slot, (0 if way == RIGHT else half), j

    def early(way, j):
        slot = 5 + j if way == RIGHT else 3 - j
        return slot, (half if way == RIGHT else 0), 4 + j

    def pass_on(way, which, j):
        slot, row0, idx = which(way, j)

        def one(s, _):
            at = pl.multiple_of(s * sub, sub)
            x = part[slot, pl.ds(row0 + at, sub), :]
            if j > 0:
                chunk(way, idx - 1, s).wait_recv()
                x = x + decode(rs_recv[way, idx - 1, pl.ds(at, sub), :])
            rs_send[way, idx, pl.ds(at, sub), :] = encode(x)
            chunk(way, idx, s).start()
            return 0

        lax.fori_loop(0, 2, one, 0)

    def loss_copy(way, j):
        slot = 4 + j if way == RIGHT else 3 - j
        idx = j if way == RIGHT else 4 + j
        return copy(
            loss_part.at[slot], loss_recv.at[idx], loss_ssem.at[idx], loss_rsem.at[idx], to[way]
        )

    def loss_on(way, j):
        slot = 4 + j if way == RIGHT else 3 - j
        idx = j if way == RIGHT else 4 + j
        if j > 0:
            loss_copy(way, j - 1).wait_recv()
            loss_part[slot] += loss_recv[idx - 1]
        loss_copy(way, j).start()

    arrive(1)
    text_copy(1).wait_recv()
    text_copy(2).start()
    text_copy(0).wait_recv()
    text_copy(2).wait_recv()
    tile(0, True)

    def pair(hop):
        def one(way, _):
            tile(hop + way * (RING - 2 * hop), False)
            return 0

        lax.fori_loop(0, 2, one, 0)

    def hops(hop, _):
        @pl.when(hop > 1)
        def _():
            arrive(hop)

        pair(hop)
        return 0

    lax.fori_loop(1, 4, hops, 0)

    pass_on(RIGHT, early, 0)
    pass_on(LEFT, early, 0)
    gather(RIGHT, 4, 0).wait_recv()
    gather(LEFT, 4, 1).wait_recv()
    tile(4, False)
    pass_on(RIGHT, late, 0)
    pass_on(LEFT, late, 0)
    loss_on(RIGHT, 0)
    loss_on(LEFT, 0)

    def text_sums(b):
        sums[b] = tn(coefs[:, pl.ds(b * rows, rows)], img[...])

    def core_copy(i):
        return copy(sums.at[1 + 2 * i], core_recv.at[i], c_ssem.at[i], c_rsem.at[i], other_core)

    text_sums(3)
    core_copy(1).start()
    text_sums(1)
    core_copy(0).start()
    text_sums(2)
    text_sums(0)

    y_copy = copy(sums.at[2], y_recv, y_ssem.at[0], y_rsem.at[0], other_y)

    def step(j):
        if j < 3:
            pass_on(RIGHT, early, j)
            pass_on(LEFT, early, j)
        pass_on(RIGHT, late, j)
        pass_on(LEFT, late, j)
        loss_on(RIGHT, j)
        if j < 3:
            loss_on(LEFT, j)

    step(1)
    core_copy(1).wait_recv()
    sums[2] += core_recv[1]
    y_copy.start()
    core_copy(0).wait_recv()
    sums[0] += core_recv[0]
    step(2)
    step(3)

    def unnormal(g, unit, inv, at, size):
        u = unit[pl.ds(at, size), :]
        along = jnp.sum(u * g, axis=1, keepdims=True)
        return (g - u * along) * (inv[pl.ds(at, size), pl.ds(0, 1)] * scale)

    y_copy.wait_recv()

    def finish_text(i, _):
        at = pl.multiple_of(i * sub, sub)
        g = sums[0, pl.ds(at, sub), :] + y_recv[pl.ds(at, sub), :]
        gt_ref[pl.ds(at, sub), :] = unnormal(g, unit_t, inv_t, at, sub)
        return 0

    lax.fori_loop(0, 4, finish_text, 0)

    def finish(piece):
        idx = (3, 6) if piece == 0 else (6, 3)

        def one(s, _):
            at = pl.multiple_of(s * sub, sub)
            row = pl.multiple_of(piece * half + s * sub, sub)
            g = part[0, pl.ds(row, sub), :]
            for way in (RIGHT, LEFT):
                chunk(way, idx[way], s).wait_recv()
                g = g + decode(rs_recv[way, idx[way], pl.ds(at, sub), :])
            gi_ref[pl.ds(row, sub), :] = unnormal(g, unit_i, inv_i, row, sub)
            return 0

        lax.fori_loop(0, 2, one, 0)

    loss_copy(RIGHT, 3).wait_recv()
    loss_copy(LEFT, 2).wait_recv()
    loss_ref[...] = loss_part[0] + loss_recv[3] + loss_recv[6]
    finish(0)
    finish(1)

    for hop in range(1, 5):
        for way in (RIGHT, LEFT):
            for piece in (0, 1):
                if hop < 4 or piece == way:
                    gather(way, hop, piece).wait_send()
    for i in range(3):
        text_copy(i).wait_send()
    for i in range(2):
        core_copy(i).wait_send()
    y_copy.wait_send()
    for j in range(4):
        loss_copy(RIGHT, j).wait_send()
        if j < 3:
            loss_copy(LEFT, j).wait_send()
    for way in (RIGHT, LEFT):
        for idx in range(7):
            for s in range(2):
                chunk(way, idx, s).wait_send()


def per_device(image_embed, text_embed, logit_scale, logit_bias):
    rows, width = image_embed.shape
    half = rows // 2
    dma = pltpu.SemaphoreType.DMA
    vmem = pl.BlockSpec(memory_space=pltpu.VMEM)
    smem = pl.BlockSpec(memory_space=pltpu.SMEM)
    loss, image_grad, text_grad = pl.pallas_call(
        kernel,
        out_shape=(
            jax.ShapeDtypeStruct((8, rows), F32),
            jax.ShapeDtypeStruct((rows, width), F32),
            jax.ShapeDtypeStruct((rows, width), F32),
        ),
        in_specs=[vmem, vmem, smem, smem],
        out_specs=(vmem, vmem, vmem),
        scratch_shapes=[
            pltpu.VMEM((RING * rows, width), BF16),
            pltpu.VMEM((QUAD * rows, width), BF16),
            pltpu.VMEM((RING, rows, width), F32),
            pltpu.VMEM((RING * rows, QUAD * rows), BF16),
            pltpu.VMEM((QUAD, rows, width), F32),
            pltpu.VMEM((2, 7, half, width), BF16),
            pltpu.VMEM((2, 7, half, width), BF16),
            pltpu.VMEM((2, rows, width), F32),
            pltpu.VMEM((rows, width), F32),
            pltpu.VMEM((rows, width), F32),
            pltpu.VMEM((rows, width), F32),
            pltpu.VMEM((rows, 128), F32),
            pltpu.VMEM((rows, 128), F32),
            pltpu.VMEM((RING, 8, rows), F32),
            pltpu.VMEM((7, 8, rows), F32),
            dma((2, 8)),
            dma((2, 8)),
            dma((2, 14)),
            dma((2, 14)),
            dma((7,)),
            dma((7,)),
            dma((3,)),
            dma((3,)),
            dma((2,)),
            dma((2,)),
            dma((1,)),
            dma((1,)),
        ],
        compiler_params=pltpu.CompilerParams(
            collective_id=0, has_side_effects=True, vmem_limit_bytes=48 * 2**20
        ),
        cost_estimate=pl.CostEstimate(
            flops=3 * 2 * 1024 * 512 * width, bytes_accessed=6 * rows * width, transcendentals=0
        ),
    )(image_embed, text_embed, logit_scale, logit_bias)
    return loss[0], image_grad, text_grad


def solution(mesh):
    placed = (P(("group", "blk"), None), P(("group", "blk"), None), P(), P())
    return jax.shard_map(
        per_device,
        mesh=mesh,
        in_specs=placed,
        out_specs=(P(("group", "blk")), P(("group", "blk"), None), P(("group", "blk"), None)),
        check_vma=False,
    )
```

time: 503 us -> 64.3 us (0.13)
  waiting for transfers between devices: 380 us -> 0 us
  matrix products: 106 us -> 0 us
  Pallas kernels: 0 us -> 57.1 us
  starting transfers between devices: 6.76 us -> 0 us
    ppermute x63 -> x0, waiting for transfers between devices: 380 us -> none  [from_behind(): return lax.ppermute(block, axis, route)]
    dot_general x96 -> x0, matrix products: 106 us -> none  [the longest x32 49.8 us: score_tile(): lax.dot_general(images, texts, (((1,), (1,)), ((), ())), preferred_elemen...]
    pallas_call x0 -> x1, Pallas kernels: none -> 57.1 us  [per_device(): pl.pallas_call(kernel, out_shape=(jax.ShapeDtypeStruct((8, rows), F32), j...]
    ppermute x63 -> x0, starting transfers between devices: 6.76 us -> none  [from_behind(): return lax.ppermute(block, axis, route)]
  transfers between devices with their start and end apart: 63 -> 0, of which waited for: 63 -> 0; matrix products, arithmetic and copies ran while one was open for 16% -> 0% of each run, Pallas kernels for 0% -> 0%
where the time goes in v1:
time: 64.3 us; the launch traced here: 63.1 us
  Pallas kernels  57.1 us (89%)
  local copies, waits for them, and re-layouts  4.06 us (6%)
  between operations  1.94 us (3%)
    pallas_call x1, Pallas kernels, per_device(): pl.pallas_call(kernel, out_shape=(jax.ShapeDtypeStruct((8, rows), F32), j...  57.1 us
    unnamed x6, local copies, waits for them, and re-layouts  3.54 us

profile of v1, /device:TPU:2, one launch (start us, length us, event | category | flops | bytes accessed | tf_op | source)
XLA Modules:
  0.0 63.1 jit_solution(2152175982074953705)
XLA Ops:
  1.9 0.0 copy-start
  1.9 1.0 %copy-done = bf16[128,1152]{1,0:T(8,128)(2,1)S(1)} copy-done((bf16[128,1152]{1,0:T(8,128)(2,1)S(1)}, bf16[128,1152]{1,0:T(8,128)(2,1)}, u32[]{:S(2)}) %copy-start) | copy-done | bytes 294936
  2.9 0.0 copy-start.1
  2.9 1.0 %copy-done.1 = bf16[128,1152]{1,0:T(8,128)(2,1)S(1)} copy-done((bf16[128,1152]{1,0:T(8,128)(2,1)S(1)}, bf16[128,1152]{1,0:T(8,128)(2,1)}, u32[]{:S(2)}) %copy-start.1) | copy-done | bytes 294936
  3.8 57.1 %shard_map.67 = (f32[8,128]{1,0:T(8,128)S(1)}, f32[128,1152]{1,0:T(8,128)S(1)}, f32[128,1152]{1,0:T(8,128)S(1)}) custom-call(bf16[128,1152]{1,0:T(8,128)(2,1)S(1)} %copy-done, bf16[128,1152]{1,0:T(8,128)(2,1)S(1)} %copy-done.1, f32[1]{0:T(128)S(6)} %copy.9.scale_ref, f32[1]{0:T(128)S(6)} %copy.10.bias_ref), custom_call_target="tpu_custom_call" | custom-call | flops 3623878656 | bytes 884736 | tf_op jit(solution)/shard_map/pallas_call | solution.py:357
  61.0 0.5 slice_bitcast_fusion
  61.5 0.8 %copy.11 = f32[128,1152]{1,0:T(8,128)} copy(f32[128,1152]{1,0:T(8,128)S(1)} %get-tuple-element.13) | data formatting | bytes 1179648
  62.3 0.8 %copy.12 = f32[128,1152]{1,0:T(8,128)} copy(f32[128,1152]{1,0:T(8,128)S(1)} %get-tuple-element.14) | data formatting | bytes 1179648
Async XLA Ops:
  1.9 1.0 %copy-start = (bf16[128,1152]{1,0:T(8,128)(2,1)S(1)}, bf16[128,1152]{1,0:T(8,128)(2,1)}, u32[]{:S(2)}) copy-start(bf16[128,1152]{1,0:T(8,128)(2,1)} %img_ref.1) | copy-start | bytes 884740
  2.9 1.0 %copy-start.1 = (bf16[128,1152]{1,0:T(8,128)(2,1)S(1)}, bf16[128,1152]{1,0:T(8,128)(2,1)}, u32[]{:S(2)}) copy-start(bf16[128,1152]{1,0:T(8,128)(2,1)} %txt_ref.1) | copy-start | bytes 884740
